TPU v7x, 256 devices: a whole 4x4x8 slice. The times are simulated.
256 devices in a mesh: zone: 64 (over y, z, core), ja: 4 (over x).
Axes of the slice: x: 4, y: 4, z: 8, core: 2. Of those that a mesh axis runs over, the one named last changes fastest.
Arguments:
- flow_state: float32 [64, 32, 5, 16, 128], P('zone', 'ja'), may hold values from -3 to 3
- forcing: float32 [64, 32, 5, 16, 128], P('zone', 'ja'), may hold values from -6 to 6
- diag_block: float32 [64, 32, 5, 5, 16, 128], P('zone', 'ja'), may hold values from -0.4 to 7.2
- lower_jac: float32 [64, 32, 5, 5, 16, 128], P('zone', 'ja'), may hold values from -4.9 to 0.2
- upper_jac: float32 [64, 32, 5, 5, 16, 128], P('zone', 'ja'), may hold values from -4.9 to 0.2
- block_inv: float32 [64, 32, 5, 5, 16, 128], P('zone', 'ja'), may hold values from -0.03 to 0.21
- east_zone: int32 [64], replicated, may hold values from 0 to 63, each once
- zone_depth: int32 [64], replicated, may hold values from 4 to 16, as said below
Outputs:
- new_state: float32 [64, 32, 5, 16, 128], P('zone', 'ja')
- last_residual: float32 [64, 32, 5, 16, 128], P('zone', 'ja')
Inputs may be any that keep to these rules, and one draw needn't show every extreme that they name: `east_zone`: a permutation of the zones. `zone_depth`: some zone has all 16 planes live.
All inputs are finite; a program needn't handle non-finite values.
Results may differ from a plain program's by a relative error of at most 0.0003.
Values sent between devices are 32-bit elements; how exact they have to be, the bound alone decides.
A program may use at most 64 MiB of HBM per device.

v0:
```python
import functools

import jax
import jax.numpy as jnp
from jax import lax
from jax.experimental import pallas as pl
from jax.experimental.pallas import tpu as pltpu
from jax.sharding import PartitionSpec as P

ITERS = 2
OMEGA = 1.2
COUPLE = 0.25
NY, NZ, NX = 4, 8, 4
MESH = pl.DeviceIdType.MESH
F32 = jnp.float32


def kernel(
    east_ref, depth_ref, flow_hbm, forc_hbm, diag_hbm, low_hbm, upp_hbm, inv_hbm,
    state_hbm, resid_hbm,
    cur, forc, diag, low, upp, inv, mm, nn, res, swp,
    mine_a, mine_b, got_a, got_b,
    gz_first, gz_second, qs, gq, halo, sb, sc, bx, cy, inflow,
    load_sem, bar_z_s, bar_z_r, sib_s, sib_r, y_s, y_r, halo_s, halo_r,
    a_s, a_r, b_s, b_r, x_s, x_r, u_s, u_r, out_sem,
):
    planes, nvar, depth_k, width = cur.shape
    rows = nvar * depth_k
    zone = lax.axis_index("zone")
    ja = lax.axis_index("ja")
    y, z, c = zone // (2 * NZ), (zone // 2) % NZ, zone % 2

    def at(dy, dz, flip):
        core = 1 - c if flip else c
        return (((y + dy) % NY) * (2 * NZ) + ((z + dz) % NZ) * 2 + core, ja)

    def along(dx):
        return (zone, (ja + dx) % NX)

    gz = (gz_first, gz_second)
    far_z = (4, 3, 5, 2, 6, 1, 7)
    far_y = (2, 1, 3)
    far_x = (2, 1, 3)
    barrier = pltpu.get_barrier_semaphore()
    partners = [at(0, d, False) for d in far_z] + [at(d, 0, False) for d in far_y]
    partners += [along(d) for d in far_x] + [at(0, 0, True)]
    for partner in partners:
        pl.semaphore_signal(barrier, 1, device_id=partner, device_id_type=MESH)

    sources = ((flow_hbm, cur), (inv_hbm, inv), (low_hbm, low), (upp_hbm, upp), (forc_hbm, forc), (diag_hbm, diag))
    loads = [pltpu.make_async_copy(src, dst, load_sem.at[i]) for i, (src, dst) in enumerate(sources)]
    for load in loads:
        load.start()

    targets = [at(d, 0, False)[0] for d in range(NY)]

    def find(w, found):
        e = east_ref[w]
        return tuple(jnp.where(e == t, w, f) for t, f in zip(targets, found))

    wests = lax.fori_loop(0, east_ref.shape[0], find, (jnp.int32(0),) * NY)
    easts = [east_ref[t] for t in targets]

    k_index = lax.broadcasted_iota(jnp.int32, (depth_k, width), 0)
    lane = lax.broadcasted_iota(jnp.int32, (depth_k, width), 1)
    live = (k_index < depth_ref[zone]).astype(F32)
    edge = ((lane == 0) | (lane == width - 1)).astype(F32)
    left_ok = (lane > 0).astype(F32)
    right_ok = (lane < width - 1).astype(F32)
    down_ok = (k_index > 0).astype(F32)
    up_ok = (k_index < depth_k - 1).astype(F32)

    def matvec(ref, j, v):
        out = ref[j, :, 0] * v[0][None]
        for col in range(1, nvar):
            out += ref[j, :, col] * v[col][None]
        return out

    def matmat(ref, j, other):
        return [matvec(ref, j, other[col]) for col in range(nvar)]

    def pack_faces(it):
        def step(m, packet):
            tile = cur[m // nvar, m % nvar]
            turned = pltpu.roll(tile, 2 * m + 1, 1)
            return jnp.where((lane == 2 * m) | (lane == 2 * m + 1), turned, packet)

        gz[it][c, z] = lax.fori_loop(0, planes * nvar, step, jnp.zeros((depth_k, width), F32))

    def z_copy(it, dz, incoming):
        slot = (z - dz) % NZ if incoming else z
        return pltpu.make_async_remote_copy(
            gz[it].at[c, z], gz[it].at[c, slot], bar_z_s.at[it, dz], bar_z_r.at[it, dz],
            device_id=at(0, dz, False), device_id_type=MESH)

    def sib_copy(it, incoming):
        side = 1 - c if incoming else c
        return pltpu.make_async_remote_copy(
            gz[it].at[c], gz[it].at[side], sib_s.at[it], sib_r.at[it],
            device_id=at(0, 0, True), device_id_type=MESH)

    def y_copy(it, dy):
        return pltpu.make_async_remote_copy(
            qs.at[it, dy], gq.at[it, dy], y_s.at[it, dy], y_r.at[it, dy],
            device_id=at(dy, 0, False), device_id_type=MESH)

    def choose(it):
        odd = lane % 2 == 1
        for dy in range(NY):
            w, e = wests[dy], easts[dy]
            west = gz[it][w % 2, (w // 2) % NZ]
            east = gz[it][e % 2, (e // 2) % NZ]
            west = jnp.where(w // (2 * NZ) == y, west, 0.0)
            east = jnp.where(e // (2 * NZ) == y, east, 0.0)
            qs[it, dy] = jnp.where(odd, pltpu.roll(west, 1, 1), pltpu.roll(east, width - 1, 1))
        for dy in far_y:
            y_copy(it, dy).start()

    def halo_copy(it, up):
        src = cur.at[0] if up else cur.at[planes - 1]
        side = 1 if up else 0
        return pltpu.make_async_remote_copy(
            src, halo.at[it, side], halo_s.at[it, side], halo_r.at[it, side],
            device_id=along(NX - 1 if up else 1), device_id_type=MESH)

    def matrix_copy(e, to, lower):
        mine, got, ss, rs = (mine_a, got_a, a_s, a_r) if lower else (mine_b, got_b, b_s, b_r)
        return pltpu.make_async_remote_copy(
            mine, got.at[e - 1], ss.at[to], rs.at[e - 1], device_id=(zone, jnp.int32(to)), device_id_type=MESH)

    def sweep_copy(it, source, to, lower):
        send, got, ss, rs = (sb, bx, x_s, x_r) if lower else (sc, cy, u_s, u_r)
        return pltpu.make_async_remote_copy(
            send.at[it], got.at[it, source], ss.at[it, to], rs.at[it, source],
            device_id=(zone, jnp.int32(to)), device_id_type=MESH)

    lower_pairs = [(0, 1), (0, 2), (0, 3), (1, 2), (1, 3), (2, 3)]
    upper_pairs = [(3, 0), (3, 1), (3, 2), (2, 1), (2, 0), (1, 0)]
    matrix_lower = [(1, 2), (1, 3), (2, 3)]
    matrix_upper = [(2, 1), (2, 0), (1, 0)]

    loads[0].wait()

    def mask_plane(j, carry):
        cur[j] = cur[j] * live[None]
        return carry

    lax.fori_loop(0, planes, mask_plane, 0)
    pack_faces(0)
    loads[1].wait()
    loads[2].wait()
    loads[3].wait()

    def premultiply(j, carry):
        for source, target in ((low, mm), (upp, nn)):
            for col in range(nvar):
                target[j, :, col] = OMEGA * matvec(inv, j, source[j, :, col])
        return carry

    lax.fori_loop(0, planes, premultiply, 0)
    mine_a[...] = mm[0]
    mine_b[...] = nn[planes - 1]

    def chain(s, carry):
        for col in range(nvar):
            mine_a[:, col] = matvec(mm, s, mine_a[:, col])
            mine_b[:, col] = matvec(nn, planes - 1 - s, mine_b[:, col])
        return carry

    lax.fori_loop(1, planes, chain, 0)
    loads[4].wait()
    loads[5].wait()
    pl.semaphore_wait(barrier, len(partners))

    for it in range(ITERS):
        if it > 0:
            pack_faces(it)
        for dz in far_z:
            z_copy(it, dz, False).start()

        @pl.when(ja > 0)
        def _():
            halo_copy(it, True).start()

        @pl.when(ja < NX - 1)
        def _():
            halo_copy(it, False).start()

        if it == 0:
            for lower, pairs in ((True, matrix_lower), (False, matrix_upper)):
                for e, to in pairs:
                    @pl.when(ja == e)
                    def _(e=e, to=to, lower=lower):
                        matrix_copy(e, to, lower).start()

        @pl.when(ja > 0)
        def _():
            halo_copy(it, False).wait_recv()

        @pl.when(ja == 0)
        def _():
            halo[it, 0] = jnp.zeros((nvar, depth_k, width), F32)

        @pl.when(ja < NX - 1)
        def _():
            halo_copy(it, True).wait_recv()

        @pl.when(ja == NX - 1)
        def _():
            halo[it, 1] = jnp.zeros((nvar, depth_k, width), F32)

        def residual(j, below):
            here = cur[j]
            above = jnp.where(j == planes - 1, halo[it, 1], cur[jnp.minimum(j + 1, planes - 1)])
            flat = here.reshape(rows, width)

            def shifted(by, axis, size, mask):
                return pltpu.roll(flat, by % size, axis).reshape(here.shape) * mask[None]

            beside = shifted(1, 1, width, left_ok) + shifted(-1, 1, width, right_ok)
            beside += shifted(1, 0, rows, down_ok) + shifted(-1, 0, rows, up_ok)
            applied = matvec(diag, j, here) - matvec(low, j, below) - matvec(upp, j, above) - COUPLE * beside
            res[j] = live[None] * (forc[j] - applied)
            return here

        lax.fori_loop(0, planes, residual, halo[it, 0])

        for dz in far_z:
            z_copy(it, dz, True).wait_recv()
        sib_copy(it, False).start()
        sib_copy(it, True).wait_recv()
        choose(it)
        for dy in far_y:
            y_copy(it, dy).wait_recv()
        ghosts = qs[it, 0] + gq[it, 1] + gq[it, 2] + gq[it, 3]
        ghost_weight = COUPLE * live * edge

        def add_ghost(m, carry):
            j, v = m // nvar, m % nvar
            res[j, v] += ghost_weight * pltpu.roll(ghosts, width - 1 - 2 * m, 1)
            return carry

        lax.fori_loop(0, planes * nvar, add_ghost, 0)
        if it == ITERS - 1:
            out_res = pltpu.make_async_copy(res, resid_hbm, out_sem.at[0])
            out_res.start()

        def solve(j, before):
            swp[j] = matvec(inv, j, res[j])
            swp[j] += matvec(mm, j, before)
            return swp[j]

        sb[it] = lax.fori_loop(0, planes, solve, jnp.zeros((nvar, depth_k, width), F32))
        for source, to in lower_pairs:
            @pl.when(ja == source)
            def _(source=source, to=to):
                sweep_copy(it, source, to, True).start()
        if it == 0:
            for lower, pairs in ((True, matrix_lower), (False, matrix_upper)):
                for e, to in pairs:
                    @pl.when(ja == to)
                    def _(e=e, to=to, lower=lower):
                        matrix_copy(e, to, lower).wait_recv()
        for source, to in lower_pairs:
            @pl.when(ja == to)
            def _(source=source, to=to):
                sweep_copy(it, source, to, True).wait_recv()

        @pl.when(ja == 0)
        def _():
            inflow[...] = jnp.zeros((nvar, depth_k, width), F32)

        @pl.when(ja > 0)
        def _():
            inflow[...] = bx[it, 0]

        for e in (1, 2):
            @pl.when(ja > e)
            def _(e=e):
                inflow[...] = bx[it, e] + matvec(got_a, e - 1, inflow[...])

        def lower_fix(j, change):
            change = matvec(mm, j, change)
            swp[j] += change
            return change

        lax.fori_loop(0, planes, lower_fix, inflow[...])

        def upper_step(s, after):
            j = planes - 1 - s
            swp[j] += matvec(nn, j, after)
            return swp[j]

        sc[it] = lax.fori_loop(0, planes, upper_step, jnp.zeros((nvar, depth_k, width), F32))
        for source, to in upper_pairs:
            @pl.when(ja == source)
            def _(source=source, to=to):
                sweep_copy(it, source, to, False).start()
        for source, to in upper_pairs:
            @pl.when(ja == to)
            def _(source=source, to=to):
                sweep_copy(it, source, to, False).wait_recv()

        @pl.when(ja == NX - 1)
        def _():
            inflow[...] = jnp.zeros((nvar, depth_k, width), F32)

        @pl.when(ja < NX - 1)
        def _():
            inflow[...] = cy[it, NX - 1]

        for e in (2, 1):
            @pl.when(ja < e)
            def _(e=e):
                inflow[...] = cy[it, e] + matvec(got_b, e - 1, inflow[...])

        @pl.when(ja > 0)
        def _():
            halo_copy(it, True).wait_send()

        @pl.when(ja < NX - 1)
        def _():
            halo_copy(it, False).wait_send()

        def upper_fix(s, change):
            j = planes - 1 - s
            change = matvec(nn, j, change)
            cur[j] += swp[j] + change
            return change

        lax.fori_loop(0, planes, upper_fix, inflow[...])

    out_state = pltpu.make_async_copy(cur, state_hbm, out_sem.at[1])
    out_state.start()
    for it in range(ITERS):
        for dz in far_z:
            z_copy(it, dz, False).wait_send()
        sib_copy(it, False).wait_send()
        for dy in far_y:
            y_copy(it, dy).wait_send()
        for lower, pairs in ((True, lower_pairs), (False, upper_pairs)):
            for source, to in pairs:
                @pl.when(ja == source)
                def _(source=source, to=to, lower=lower):
                    sweep_copy(it, source, to, lower).wait_send()
    for lower, pairs in ((True, matrix_lower), (False, matrix_upper)):
        for e, to in pairs:
            @pl.when(ja == e)
            def _(e=e, to=to, lower=lower):
                matrix_copy(e, to, lower).wait_send()
    out_res.wait()
    out_state.wait()


def per_device(flow_state, forcing, diag_block, lower_jac, upper_jac, block_inv, east_zone, zone_depth):
    planes, nvar, depth_k, width = flow_state.shape[1:]
    vec = (nvar, depth_k, width)
    mat = (nvar,) + vec
    dma = pltpu.SemaphoreType.DMA
    state, resid = pl.pallas_call(
        kernel,
        out_shape=[jax.ShapeDtypeStruct((planes,) + vec, F32)] * 2,
        in_specs=[pl.BlockSpec(memory_space=pltpu.SMEM)] * 2 + [pl.BlockSpec(memory_space=pl.ANY)] * 6,
        out_specs=[pl.BlockSpec(memory_space=pl.ANY)] * 2,
        scratch_shapes=[
            pltpu.VMEM((planes,) + vec, F32), pltpu.VMEM((planes,) + vec, F32),
            pltpu.VMEM((planes,) + mat, F32), pltpu.VMEM((planes,) + mat, F32),
            pltpu.VMEM((planes,) + mat, F32), pltpu.VMEM((planes,) + mat, F32),
            pltpu.VMEM((planes,) + mat, F32), pltpu.VMEM((planes,) + mat, F32),
            pltpu.VMEM((planes,) + vec, F32), pltpu.VMEM((planes,) + vec, F32),
            pltpu.VMEM(mat, F32), pltpu.VMEM(mat, F32),
            pltpu.VMEM((2,) + mat, F32), pltpu.VMEM((2,) + mat, F32),
            pltpu.VMEM((2, NZ, depth_k, width), F32), pltpu.VMEM((2, NZ, depth_k, width), F32),
            pltpu.VMEM((ITERS, NY, depth_k, width), F32), pltpu.VMEM((ITERS, NY, depth_k, width), F32),
            pltpu.VMEM((ITERS, 2) + vec, F32),
            pltpu.VMEM((ITERS,) + vec, F32), pltpu.VMEM((ITERS,) + vec, F32),
            pltpu.VMEM((ITERS, NX) + vec, F32), pltpu.VMEM((ITERS, NX) + vec, F32),
            pltpu.VMEM(vec, F32),
            dma((6,)), dma((ITERS, NZ)), dma((ITERS, NZ)), dma((ITERS,)), dma((ITERS,)),
            dma((ITERS, NY)), dma((ITERS, NY)), dma((ITERS, 2)), dma((ITERS, 2)),
            dma((NX,)), dma((2,)), dma((NX,)), dma((2,)),
            dma((ITERS, NX)), dma((ITERS, NX)), dma((ITERS, NX)), dma((ITERS, NX)), dma((2,)),
        ],
        compiler_params=pltpu.CompilerParams(
            collective_id=0, has_side_effects=True, vmem_limit_bytes=48 * 2**20),
        name="ssor",
    )(east_zone, zone_depth, flow_state[0], forcing[0], diag_block[0], lower_jac[0], upper_jac[0], block_inv[0])
    return state[None], resid[None]


def solution(mesh):
    vec = P("zone", "ja", None, None, None)
    mat = P("zone", "ja", None, None, None, None)
    return jax.shard_map(
        per_device,
        mesh=mesh,
        in_specs=(vec, vec, mat, mat, mat, mat, P(), P()),
        out_specs=(vec, vec),
        check_vma=False,
    )
```

profile of v0, /device:TPU:1, one launch (start us, length us, event | category | flops | bytes accessed | tf_op | source)
XLA Modules:
  0.0 67.4 jit_solution(14791092881019297662)
XLA Ops:
  0.6 0.0 copy-start
  0.6 1.4 %copy-done = f32[1,8,5,5,16,128]{5,4,3,2,1,0:T(8,128)S(1)} copy-done((f32[1,8,5,5,16,128]{5,4,3,2,1,0:T(8,128)S(1)}, f32[1,8,5,5,16,128]{5,4,3,2,1,0:T(8,128)}, u32[]{:S(2)}) %copy-start) | copy-done | bytes 1638424
  2.1 0.0 copy-start.1
  2.1 1.4 %copy-done.1 = f32[1,8,5,5,16,128]{5,4,3,2,1,0:T(8,128)S(1)} copy-done((f32[1,8,5,5,16,128]{5,4,3,2,1,0:T(8,128)S(1)}, f32[1,8,5,5,16,128]{5,4,3,2,1,0:T(8,128)}, u32[]{:S(2)}) %copy-start.1) | copy-done | bytes 1638424
  3.5 0.0 copy-start.2
  3.5 1.0 %copy-done.2 = f32[1,8,5,16,128]{4,3,2,1,0:T(8,128)S(1)} copy-done((f32[1,8,5,16,128]{4,3,2,1,0:T(8,128)S(1)}, f32[1,8,5,16,128]{4,3,2,1,0:T(8,128)}, u32[]{:S(2)}) %copy-start.2) | copy-done | bytes 327704
  4.5 0.0 copy-start.3
  4.5 1.0 %copy-done.3 = f32[1,8,5,16,128]{4,3,2,1,0:T(8,128)S(1)} copy-done((f32[1,8,5,16,128]{4,3,2,1,0:T(8,128)S(1)}, f32[1,8,5,16,128]{4,3,2,1,0:T(8,128)}, u32[]{:S(2)}) %copy-start.3) | copy-done | bytes 327704
  5.4 0.0 copy-start.4
  5.4 0.7 copy-done.4
  6.1 0.0 copy-start.5
  6.1 0.7 copy-done.5
  6.8 59.2 %ssor.1 = (f32[8,5,16,128]{3,2,1,0:T(8,128)S(1)}, f32[8,5,16,128]{3,2,1,0:T(8,128)S(1)}) custom-call(s32[64]{0:T(128)S(1)} %copy-done.4, s32[64]{0:T(128)S(1)} %copy-done.5, f32[8,5,16,128]{3,2,1,0:T(8,128)S(1)} %bitcast.12, f32[8,5,16,128]{3,2,1,0:T(8,128)S(1)} %bitcast.13, f32[8,5,5,16,128]{4,3,2,1,0:T(8,128)S(1)} %bitcast.8, ...), custom_call_target="tpu_custom_call" | custom-call | tf_op jit(solution)/shard_map/ssor/pallas_call | solution.py:360
  66.0 0.7 %copy.12 = f32[1,8,5,16,128]{4,3,2,1,0:T(8,128)} copy(f32[1,8,5,16,128]{4,3,2,1,0:T(8,128)S(1)} %bitcast.11) | data formatting | bytes 655360
  66.7 0.7 %copy.13 = f32[1,8,5,16,128]{4,3,2,1,0:T(8,128)} copy(f32[1,8,5,16,128]{4,3,2,1,0:T(8,128)S(1)} %bitcast.10) | data formatting | bytes 655360
Async XLA Ops:
  0.6 1.4 %copy-start = (f32[1,8,5,5,16,128]{5,4,3,2,1,0:T(8,128)S(1)}, f32[1,8,5,5,16,128]{5,4,3,2,1,0:T(8,128)}, u32[]{:S(2)}) copy-start(f32[1,8,5,5,16,128]{5,4,3,2,1,0:T(8,128)} %param.10) | copy-start | bytes 4915204
  2.1 1.4 %copy-start.1 = (f32[1,8,5,5,16,128]{5,4,3,2,1,0:T(8,128)S(1)}, f32[1,8,5,5,16,128]{5,4,3,2,1,0:T(8,128)}, u32[]{:S(2)}) copy-start(f32[1,8,5,5,16,128]{5,4,3,2,1,0:T(8,128)} %param.11) | copy-start | bytes 4915204
  3.5 1.0 %copy-start.2 = (f32[1,8,5,16,128]{4,3,2,1,0:T(8,128)S(1)}, f32[1,8,5,16,128]{4,3,2,1,0:T(8,128)}, u32[]{:S(2)}) copy-start(f32[1,8,5,16,128]{4,3,2,1,0:T(8,128)} %param.8) | copy-start | bytes 983044
  4.5 1.0 %copy-start.3 = (f32[1,8,5,16,128]{4,3,2,1,0:T(8,128)S(1)}, f32[1,8,5,16,128]{4,3,2,1,0:T(8,128)}, u32[]{:S(2)}) copy-start(f32[1,8,5,16,128]{4,3,2,1,0:T(8,128)} %param.9) | copy-start | bytes 983044
  5.4 0.7 copy-start.4
  6.1 0.7 copy-start.5
where the time goes:
time: 67.7 us; the launch traced here: 67.4 us
  Pallas kernels  59.2 us (87%)
  local copies, waits for them, and re-layouts  7.56 us (11%)
    pallas_call x1, Pallas kernels, per_device(): pl.pallas_call(kernel, out_shape=[jax.ShapeDtypeStruct((planes,) + vec, F...  59.2 us
    unnamed x14, local copies, waits for them, and re-layouts  7.56 us

commit v1 on v0

v1 whole, which is shorter than its diff:
```python
import jax
import jax.numpy as jnp
from jax import lax
from jax.experimental import pallas as pl
from jax.experimental.pallas import tpu as pltpu
from jax.sharding import PartitionSpec as P

ITERS = 2
OMEGA = 1.2
COUPLE = 0.25
NY, NZ, NX = 4, 8, 4
MESH = pl.DeviceIdType.MESH
F32 = jnp.float32
FACE_STEPS = ((2, 1), (2, 0), (1, 1), (3, 1), (1, 0), (3, 0), (0, 1))
Z_STEPS = (4, 3, 5, 2, 6, 1, 7)
JA_STEPS = (2, 1, 3)
LOWER_PAIRS = ((0, 2), (1, 3), (0, 1), (1, 2), (2, 3), (0, 3))
UPPER_PAIRS = ((3, 1), (2, 0), (3, 2), (2, 1), (1, 0), (3, 0))
LOWER_MATS = ((1, 2), (2, 3), (1, 3))
UPPER_MATS = ((2, 1), (1, 0), (2, 0))


def kernel(
    east_hbm, depth_hbm, flow_hbm, forc_hbm, diag_hbm, low_hbm, upp_hbm, inv_hbm,
    state_hbm, resid_hbm,
    east_ref, depth_ref, cur, forc, diag, low, upp, inv,
    mm, nn, pp, rr, hh, res, gres, sol, got_a, got_b,
    edge_pack, edge_mat, face0, face1, chosen, ghost_in, halo,
    sb, sc, bx, cy, xin, yin, small, small_vec,
    load_sem, face_s, face_r, z_s, z_r, halo_s, halo_r,
    a_s, a_r, b_s, b_r, e_s, e_r, x_s, x_r, u_s, u_r, g_s, g_r, out_sem,
):
    planes, nvar, depth_k, width = cur.shape
    rows = nvar * depth_k
    last = planes - 1
    vec = (nvar, depth_k, width)
    faces = (face0, face1)
    zone = lax.axis_index("zone")
    ja = lax.axis_index("ja")
    y, z, c = zone // (2 * NZ), (zone // 2) % NZ, zone % 2

    def at(dy, dz, flip):
        core = 1 - c if flip else c
        return (((y + dy) % NY) * (2 * NZ) + ((z + dz) % NZ) * 2 + core, ja)

    def along(dx):
        return (zone, (ja + dx) % NX)

    def on(device):
        return (zone, jnp.int32(device))

    barrier = pltpu.get_barrier_semaphore()
    partners = [at(dy, 0, flip) for dy, flip in FACE_STEPS] + [at(0, d, 0) for d in Z_STEPS]
    partners += [along(d) for d in JA_STEPS]
    for partner in partners:
        pl.semaphore_signal(barrier, 1, device_id=partner, device_id_type=MESH)

    sources = (
        (east_hbm, east_ref), (depth_hbm, depth_ref), (flow_hbm, cur), (inv_hbm, inv),
        (low_hbm, low), (upp_hbm, upp), (diag_hbm, diag), (forc_hbm, forc))
    loads = [pltpu.make_async_copy(src, dst, load_sem.at[i]) for i, (src, dst) in enumerate(sources)]
    for load in loads:
        load.start()

    k_index = lax.broadcasted_iota(jnp.int32, (depth_k, width), 0)
    lane = lax.broadcasted_iota(jnp.int32, (depth_k, width), 1)
    edge = ((lane == 0) | (lane == width - 1)).astype(F32)
    left_ok = (lane > 0).astype(F32)
    right_ok = (lane < width - 1).astype(F32)
    down_ok = (k_index > 0).astype(F32)
    up_ok = (k_index < depth_k - 1).astype(F32)
    odd = lane % 2 == 1

    def remote(src, dst, ss, rs, device):
        return pltpu.make_async_remote_copy(src, dst, ss, rs, device_id=device, device_id_type=MESH)

    def times(mat, v):
        out = mat[:, 0] * v[0][None]
        for col in range(1, nvar):
            out += mat[:, col] * v[col][None]
        return out

    def pack(tile, m, packet):
        turned = pltpu.roll(tile, 2 * m + 1, 1)
        return jnp.where((lane == 2 * m) | (lane == 2 * m + 1), turned, packet)

    def unpack(packet, m):
        return pltpu.roll(packet, width - 1 - 2 * m, 1)

    def pack_faces(it):
        packet = jnp.zeros((depth_k, width), F32)
        for m in range(planes * nvar):
            packet = pack(cur[m // nvar, m % nvar], m, packet)
        faces[it][c, y] = packet

    def face_copy(it, i, incoming):
        dy, flip = FACE_STEPS[i]
        slot = faces[it].at[1 - c if flip else c, (y - dy) % NY] if incoming else faces[it].at[c, y]
        return remote(faces[it].at[c, y], slot, face_s.at[it, i], face_r.at[it, i], at(dy, 0, flip))

    def z_copy(it, dz):
        return remote(chosen.at[it, dz], ghost_in.at[it, dz], z_s.at[it, dz], z_r.at[it, dz], at(0, dz, 0))

    def halo_copy(it, up):
        side = 1 if up else 0
        return remote(
            cur.at[0 if up else last], halo.at[it, side], halo_s.at[it, side], halo_r.at[it, side],
            along(NX - 1 if up else 1))

    def matrix_copy(e, to, lower):
        mine, got, ss, rs = (pp.at[last], got_a, a_s, a_r) if lower else (rr.at[0], got_b, b_s, b_r)
        return remote(mine, got.at[e - 1], ss.at[to], rs.at[e - 1], on(to))

    def edge_copy(i):
        dx = JA_STEPS[i]
        return remote(edge_pack.at[ja], edge_pack.at[ja], e_s.at[i], e_r.at[i], along(dx))

    def edge_arrival(i):
        source = (ja - JA_STEPS[i]) % NX
        return remote(edge_pack.at[source], edge_pack.at[source], e_s.at[i], e_r.at[i], along(JA_STEPS[i]))

    def small_copy(it, i, incoming):
        dx = JA_STEPS[i]
        slot = (ja - dx) % NX if incoming else ja
        return remote(small.at[it, ja], small.at[it, slot], g_s.at[it, i], g_r.at[it, i], along(dx))

    def sweep_copy(it, source, to, lower):
        send, got, ss, rs = (sb, bx, x_s, x_r) if lower else (sc, cy, u_s, u_r)
        return remote(send.at[it], got.at[it, source], ss.at[it, to], rs.at[it, source], on(to))

    def residual_bulk(live):
        def step(j, below):
            here = cur[j]
            above = jnp.where(j == last, 0.0, cur[jnp.minimum(j + 1, last)])
            flat = here.reshape(rows, width)

            def shifted(by, axis, size, mask):
                return pltpu.roll(flat, by % size, axis).reshape(vec) * mask[None]

            beside = shifted(1, 1, width, left_ok) + shifted(-1, 1, width, right_ok)
            beside += shifted(1, 0, rows, down_ok) + shifted(-1, 0, rows, up_ok)
            applied = times(diag[j], here) - times(low[j], below) - times(upp[j], above) - COUPLE * beside
            res[j] = live[None] * (forc[j] - applied)
            return here

        lax.fori_loop(0, planes, step, jnp.zeros(vec, F32))

        def start(j, carry):
            sol[j] = times(inv[j], res[j])
            return carry

        lax.fori_loop(1, last, start, 0, unroll=2)

    loads[0].wait()
    loads[1].wait()
    targets = [at(0, d, 0)[0] for d in range(NZ)]

    def find(w, found):
        e = east_ref[w]
        return tuple(jnp.where(e == t, w, f) for t, f in zip(targets, found))

    wests = lax.fori_loop(0, NY * NZ * 2, find, (jnp.int32(0),) * NZ)
    easts = [east_ref[t] for t in targets]
    live = (k_index < depth_ref[zone]).astype(F32)
    ghost_weight = COUPLE * live * edge

    loads[2].wait()

    def mask_plane(j, carry):
        cur[j] = cur[j] * live[None]
        return carry

    lax.fori_loop(0, planes, mask_plane, 0, unroll=2)
    pack_faces(0)
    for i in (3, 4, 5):
        loads[i].wait()

    def premultiply(j, carry):
        for source, target in ((low, mm), (upp, nn)):
            for col in range(nvar):
                target[j, :, col] = OMEGA * times(inv[j], source[j, :, col])
        return carry

    lax.fori_loop(0, planes, premultiply, 0)
    pp[0] = mm[0]
    rr[last] = nn[last]

    def products(s, carry):
        j = last - s
        for col in range(nvar):
            pp[s, :, col] = times(mm[s], pp[s - 1, :, col])
            rr[j, :, col] = times(nn[j], rr[j + 1, :, col])
        return carry

    lax.fori_loop(1, planes, products, 0)
    hh[last] = pp[last]

    def through(s, carry):
        j = last - s
        for col in range(nvar):
            hh[j, :, col] = pp[j, :, col] + times(nn[j], hh[j + 1, :, col])
        return carry

    lax.fori_loop(1, planes, through, 0)
    packets = [jnp.zeros((depth_k, width), F32)] * 3
    for row in range(nvar):
        for col in range(nvar):
            for i, product in enumerate((pp.at[last], rr.at[0], hh.at[0])):
                packets[i] = pack(product[row, col], row * nvar + col, packets[i])
    for i in range(3):
        edge_pack[ja, i] = packets[i]
    loads[6].wait()
    loads[7].wait()
    residual_bulk(live)
    pl.semaphore_wait(barrier, len(partners))

    for it in range(ITERS):
        for i in range(len(FACE_STEPS)):
            face_copy(it, i, False).start()

        @pl.when(ja > 0)
        def _():
            halo_copy(it, True).start()

        @pl.when(ja < NX - 1)
        def _():
            halo_copy(it, False).start()

        if it == 0:
            for i in range(len(JA_STEPS)):
                edge_copy(i).start()
            for lower, pairs in ((True, LOWER_MATS), (False, UPPER_MATS)):
                for e, to in pairs:
                    @pl.when(ja == e)
                    def _(e=e, to=to, lower=lower):
                        matrix_copy(e, to, lower).start()
        else:
            residual_bulk(live)

        @pl.when(ja > 0)
        def _():
            halo_copy(it, False).wait_recv()
            res[0] += live[None] * times(low[0], halo[it, 0])

        @pl.when(ja < NX - 1)
        def _():
            halo_copy(it, True).wait_recv()
            res[last] += live[None] * times(upp[last], halo[it, 1])

        sol[0] = times(inv[0], res[0])
        sol[last] = times(inv[last], res[last])

        def lower_step(j, before):
            value = sol[j] + times(mm[j], before)
            sol[j] = value
            return value

        def upper_step(s, after):
            j = last - s
            value = sol[j] + times(nn[j], after)
            sol[j] = value
            return value

        sb[it] = lax.fori_loop(1, planes, lower_step, sol[0], unroll=True)
        for source, to in LOWER_PAIRS:
            @pl.when(ja == source)
            def _(source=source, to=to):
                sweep_copy(it, source, to, True).start()
        lax.fori_loop(1, planes, upper_step, sol[last], unroll=True)

        for i in range(len(FACE_STEPS)):
            face_copy(it, i, True).wait_recv()
        for dz in Z_STEPS + (0,):
            w, e = wests[dz], easts[dz]
            west = faces[it][w % 2, w // (2 * NZ)]
            east = faces[it][e % 2, e // (2 * NZ)]
            west = jnp.where((w // 2) % NZ == z, west, 0.0)
            east = jnp.where((e // 2) % NZ == z, east, 0.0)
            chosen[it, dz] = jnp.where(odd, pltpu.roll(west, 1, 1), pltpu.roll(east, width - 1, 1))
            if dz:
                z_copy(it, dz).start()

        if it == 0:
            for i in range(len(JA_STEPS)):
                edge_arrival(i).wait_recv()

            def spread(m, carry):
                row, col = m // nvar, m % nvar
                for e in (1, 2, 3):
                    for i in range(3):
                        if e < 3 or i == 2:
                            edge_mat[e, i, row, col] = unpack(edge_pack[e, i], m)
                return carry

            lax.fori_loop(0, nvar * nvar, spread, 0, unroll=5)
            for lower, pairs in ((True, LOWER_MATS), (False, UPPER_MATS)):
                for e, to in pairs:
                    @pl.when(ja == to)
                    def _(e=e, to=to, lower=lower):
                        matrix_copy(e, to, lower).wait_recv()

        for source, to in LOWER_PAIRS:
            @pl.when(ja == to)
            def _(source=source, to=to):
                sweep_copy(it, source, to, True).wait_recv()

        @pl.when(ja == 0)
        def _():
            xin[...] = jnp.zeros(vec, F32)

        @pl.when(ja > 0)
        def _():
            xin[...] = bx[it, 0]

        for e in (1, 2):
            @pl.when(ja > e)
            def _(e=e):
                xin[...] = bx[it, e] + times(got_a[e - 1], xin[...])

        sc[it] = sol[0] + times(hh[0], xin[...])
        for source, to in UPPER_PAIRS:
            @pl.when(ja == source)
            def _(source=source, to=to):
                sweep_copy(it, source, to, False).start()

        for dz in Z_STEPS:
            z_copy(it, dz).wait_recv()
        ghosts = chosen[it, 0]
        for dz in Z_STEPS:
            ghosts += ghost_in[it, dz]
        for m in range(planes * nvar):
            gres[m // nvar, m % nvar] = ghost_weight * unpack(ghosts, m)

        def ghost_start(j, carry):
            mine = gres[j]
            res[j] += mine
            gres[j] = times(inv[j], mine)
            return carry

        lax.fori_loop(0, planes, ghost_start, 0, unroll=4)
        if it == ITERS - 1:
            out_res = pltpu.make_async_copy(res, resid_hbm, out_sem.at[0])
            out_res.start()

        def ghost_lower(j, before):
            value = gres[j] + times(mm[j], before)
            gres[j] = value
            return value

        def ghost_upper(s, after):
            j = last - s
            value = gres[j] + times(nn[j], after)
            sol[j] += value
            return value

        bottom = lax.fori_loop(1, planes, ghost_lower, gres[0], unroll=True)
        sol[last] += bottom
        top = lax.fori_loop(1, planes, ghost_upper, bottom, unroll=True)
        packet = jnp.zeros((depth_k, width), F32)
        for v in range(nvar):
            packet = pack(bottom[v], v, packet)
            packet = pack(top[v], nvar + v, packet)
        small[it, ja] = packet
        for i in range(len(JA_STEPS)):
            small_copy(it, i, False).start()

        for source, to in UPPER_PAIRS:
            @pl.when(ja == to)
            def _(source=source, to=to):
                sweep_copy(it, source, to, False).wait_recv()

        @pl.when(ja == NX - 1)
        def _():
            yin[...] = jnp.zeros(vec, F32)

        @pl.when(ja < NX - 1)
        def _():
            yin[...] = cy[it, NX - 1]

        for e in (2, 1):
            @pl.when(ja < e)
            def _(e=e):
                yin[...] = cy[it, e] + times(got_b[e - 1], yin[...])

        @pl.when(ja > 0)
        def _():
            halo_copy(it, True).wait_send()

        @pl.when(ja < NX - 1)
        def _():
            halo_copy(it, False).wait_send()

        def raise_plane(j, carry):
            cur[j] += sol[j] + times(hh[j], xin[...]) + times(rr[j], yin[...])
            return carry

        lax.fori_loop(0, planes, raise_plane, 0, unroll=2)

        for i in range(len(JA_STEPS)):
            small_copy(it, i, True).wait_recv()
        for e in range(NX):
            for v in range(nvar):
                if e < NX - 1:
                    small_vec[e, v] = edge * unpack(small[it, e], v)
                if e > 0:
                    small_vec[e, nvar + v] = edge * unpack(small[it, e], nvar + v)
        low_end, high_end = pl.ds(0, nvar), pl.ds(nvar, nvar)
        x1 = small_vec[0, low_end]
        x2 = small_vec[1, low_end] + times(edge_mat[1, 0], x1)
        x3 = small_vec[2, low_end] + times(edge_mat[2, 0], x2)
        y2 = small_vec[3, high_end] + times(edge_mat[3, 2], x3)
        y1 = small_vec[2, high_end] + times(edge_mat[2, 2], x2) + times(edge_mat[2, 1], y2)
        y0 = small_vec[1, high_end] + times(edge_mat[1, 2], x1) + times(edge_mat[1, 1], y1)
        xin[...] = jnp.where(ja == 0, 0.0, jnp.where(ja == 1, x1, jnp.where(ja == 2, x2, x3)))
        yin[...] = jnp.where(ja == 3, 0.0, jnp.where(ja == 2, y2, jnp.where(ja == 1, y1, y0)))

        def raise_edges(j, carry):
            cur[j] += times(hh[j], xin[...]) + times(rr[j], yin[...])
            return carry

        lax.fori_loop(0, planes, raise_edges, 0, unroll=4)
        if it < ITERS - 1:
            pack_faces(it + 1)

    out_state = pltpu.make_async_copy(cur, state_hbm, out_sem.at[1])
    out_state.start()
    for it in range(ITERS):
        for i in range(len(FACE_STEPS)):
            face_copy(it, i, False).wait_send()
        for dz in Z_STEPS:
            z_copy(it, dz).wait_send()
        for i in range(len(JA_STEPS)):
            small_copy(it, i, False).wait_send()
        for lower, pairs in ((True, LOWER_PAIRS), (False, UPPER_PAIRS)):
            for source, to in pairs:
                @pl.when(ja == source)
                def _(source=source, to=to, lower=lower):
                    sweep_copy(it, source, to, lower).wait_send()
    for i in range(len(JA_STEPS)):
        edge_copy(i).wait_send()
    for lower, pairs in ((True, LOWER_MATS), (False, UPPER_MATS)):
        for e, to in pairs:
            @pl.when(ja == e)
            def _(e=e, to=to, lower=lower):
                matrix_copy(e, to, lower).wait_send()
    out_res.wait()
    out_state.wait()


def per_device(flow_state, forcing, diag_block, lower_jac, upper_jac, block_inv, east_zone, zone_depth):
    planes, nvar, depth_k, width = flow_state.shape[1:]
    tile = (depth_k, width)
    vec = (nvar,) + tile
    mat = (nvar,) + vec
    dma = pltpu.SemaphoreType.DMA

    def vmem(*shape):
        return pltpu.VMEM(shape, F32)

    ints = pltpu.SMEM(east_zone.shape, jnp.int32)
    state, resid = pl.pallas_call(
        kernel,
        out_shape=[jax.ShapeDtypeStruct((planes,) + vec, F32)] * 2,
        in_specs=[pl.BlockSpec(memory_space=pltpu.HBM)] * 8,
        out_specs=[pl.BlockSpec(memory_space=pltpu.HBM)] * 2,
        scratch_shapes=[ints, ints]
        + [vmem(planes, *vec)] * 2 + [vmem(planes, *mat)] * 4
        + [vmem(planes, *mat)] * 5 + [vmem(planes, *vec)] * 3 + [vmem(2, *mat)] * 2
        + [vmem(NX, 3, *tile), vmem(NX, 3, *mat), vmem(2, NY, *tile), vmem(2, NY, *tile)]
        + [vmem(ITERS, NZ, *tile)] * 2 + [vmem(ITERS, 2, *vec)]
        + [vmem(ITERS, *vec)] * 2 + [vmem(ITERS, NX, *vec)] * 2 + [vmem(*vec)] * 2
        + [vmem(ITERS, NX, *tile), vmem(NX, 2 * nvar, *tile)]
        + [dma((8,)), dma((ITERS, 7)), dma((ITERS, 7)), dma((ITERS, NZ)), dma((ITERS, NZ)), dma((ITERS, 2)), dma((ITERS, 2))]
        + [dma((NX,)), dma((2,)), dma((NX,)), dma((2,)), dma((3,)), dma((3,))]
        + [dma((ITERS, NX))] * 4 + [dma((ITERS, 3))] * 2 + [dma((2,))],
        compiler_params=pltpu.CompilerParams(
            collective_id=0, has_side_effects=True, vmem_limit_bytes=64 * 2**20 - 2**17),
        name="ssor",
    )(east_zone, zone_depth, flow_state[0], forcing[0], diag_block[0], lower_jac[0], upper_jac[0], block_inv[0])
    return state[None], resid[None]


def solution(mesh):
    vec = P("zone", "ja", None, None, None)
    mat = P("zone", "ja", None, None, None, None)
    return jax.shard_map(
        per_device,
        mesh=mesh,
        in_specs=(vec, vec, mat, mat, mat, mat, P(), P()),
        out_specs=(vec, vec),
        check_vma=False,
    )
```

time: 67.7 us -> 50.6 us (0.75)
  Pallas kernels: 59.2 us -> 46.3 us
  local copies, waits for them, and re-layouts: 7.56 us -> 3.44 us
    pallas_call x1, Pallas kernels: 59.2 us -> 46.3 us  [per_device(): pl.pallas_call(kernel, out_shape=[jax.ShapeDtypeStruct((planes,) + vec, F...]
    unnamed x14 -> x2, local copies, waits for them, and re-layouts: 7.56 us -> 3.44 us
where the time goes in v1:
time: 50.6 us; the launch traced here: 50.4 us
  Pallas kernels  46.3 us (92%)
  local copies, waits for them, and re-layouts  3.44 us (7%)
  between operations  0.64 us (1%)
    pallas_call x1, Pallas kernels, per_device(): pl.pallas_call(kernel, out_shape=[jax.ShapeDtypeStruct((planes,) + vec, F...  46.3 us
    unnamed x2, local copies, waits for them, and re-layouts  3.44 us

profile of v1, /device:TPU:1, one launch (start us, length us, event | category | flops | bytes accessed | tf_op | source)
XLA Modules:
  0.0 50.4 jit_solution(13983477599087607577)
XLA Ops:
  0.6 46.3 %ssor.1 = (f32[8,5,16,128]{3,2,1,0:T(8,128)}, f32[8,5,16,128]{3,2,1,0:T(8,128)}) custom-call(s32[64]{0:T(128)} %east_hbm.1, s32[64]{0:T(128)} %depth_hbm.1, f32[8,5,16,128]{3,2,1,0:T(8,128)} %bitcast.14, f32[8,5,16,128]{3,2,1,0:T(8,128)} %bitcast.15, f32[8,5,5,16,128]{4,3,2,1,0:T(8,128)} %bitcast.8, f32[8,5,5,16,128]{4,3,2,1,0:T(8,128)} %bitcast.9, ...), custom_call_target="tpu_custom_call" | custom-call | tf_op jit(solution)/shard_map/ssor/pallas_call | solution.py:461
  47.0 1.7 %copy.12 = f32[1,8,5,16,128]{4,3,2,1,0:T(8,128)} copy(f32[1,8,5,16,128]{4,3,2,1,0:T(8,128)} %bitcast.13) | data formatting | bytes 655360
  48.7 1.7 %copy.13 = f32[1,8,5,16,128]{4,3,2,1,0:T(8,128)} copy(f32[1,8,5,16,128]{4,3,2,1,0:T(8,128)} %bitcast.12) | data formatting | bytes 655360

commit v2 on v1

--- a/solution.py
+++ b/solution.py
@@ -14,21 +14,21 @@
 FACE_STEPS = ((2, 1), (2, 0), (1, 1), (3, 1), (1, 0), (3, 0), (0, 1))
 Z_STEPS = (4, 3, 5, 2, 6, 1, 7)
 JA_STEPS = (2, 1, 3)
-LOWER_PAIRS = ((0, 2), (1, 3), (0, 1), (1, 2), (2, 3), (0, 3))
-UPPER_PAIRS = ((3, 1), (2, 0), (3, 2), (2, 1), (1, 0), (3, 0))
-LOWER_MATS = ((1, 2), (2, 3), (1, 3))
+LOWER_PAIRS = ((0, 2, 0), (1, 3, 0), (1, 2, 0), (2, 3, 0), (0, 1, 0), (0, 3, 1))
+UPPER_PAIRS = ((3, 1, 0), (2, 0, 0), (3, 0, 0), (3, 2, 0), (2, 1, 0), (1, 0, 0))
+LOWER_MATS = ((1, 0), (1, 2), (2, 3))
 UPPER_MATS = ((2, 1), (1, 0), (2, 0))
 
 
 def kernel(
     east_hbm, depth_hbm, flow_hbm, forc_hbm, diag_hbm, low_hbm, upp_hbm, inv_hbm,
-    state_hbm, resid_hbm,
-    east_ref, depth_ref, cur, forc, diag, low, upp, inv,
-    mm, nn, pp, rr, hh, res, gres, sol, got_a, got_b,
+    cur, res,
+    east_ref, depth_ref, forc, diag, low, upp, inv,
+    mm, nn, pp, rr, hh, gres, sol, got_a, got_b,
     edge_pack, edge_mat, face0, face1, chosen, ghost_in, halo,
     sb, sc, bx, cy, xin, yin, small, small_vec,
     load_sem, face_s, face_r, z_s, z_r, halo_s, halo_r,
-    a_s, a_r, b_s, b_r, e_s, e_r, x_s, x_r, u_s, u_r, g_s, g_r, out_sem,
+    a_s, a_r, b_s, b_r, e_s, e_r, x_s, x_r, u_s, u_r, g_s, g_r,
 ):
     planes, nvar, depth_k, width = cur.shape
     rows = nvar * depth_k
@@ -108,8 +108,9 @@
             along(NX - 1 if up else 1))
 
     def matrix_copy(e, to, lower):
-        mine, got, ss, rs = (pp.at[last], got_a, a_s, a_r) if lower else (rr.at[0], got_b, b_s, b_r)
-        return remote(mine, got.at[e - 1], ss.at[to], rs.at[e - 1], on(to))
+        if lower:
+            return remote(pp.at[last], got_a, a_s.at[to // 2], a_r, on(to))
+        return remote(rr.at[0], got_b.at[e - 1], b_s.at[to], b_r.at[e - 1], on(to))
 
     def edge_copy(i):
         dx = JA_STEPS[i]
@@ -124,9 +125,36 @@
         slot = (ja - dx) % NX if incoming else ja
         return remote(small.at[it, ja], small.at[it, slot], g_s.at[it, i], g_r.at[it, i], along(dx))
 
-    def sweep_copy(it, source, to, lower):
-        send, got, ss, rs = (sb, bx, x_s, x_r) if lower else (sc, cy, u_s, u_r)
-        return remote(send.at[it], got.at[it, source], ss.at[it, to], rs.at[it, source], on(to))
+    def sweep_copy(it, source, to, through, lower):
+        send = sb.at[it, through] if lower else sc.at[it]
+        got, ss, rs = (bx, x_s, x_r) if lower else (cy, u_s, u_r)
+        return remote(send, got.at[it, source], ss.at[it, to], rs.at[it, source], on(to))
+
+    def send_matrices(lower):
+        for e, to in LOWER_MATS if lower else UPPER_MATS:
+            @pl.when(ja == e)
+            def _(e=e, to=to):
+                matrix_copy(e, to, lower).start()
+
+    def await_matrices(device, lower):
+        for e, to in LOWER_MATS if lower else UPPER_MATS:
+            if to == device:
+                @pl.when(ja == device)
+                def _(e=e):
+                    matrix_copy(e, device, lower).wait_recv()
+
+    def send_sweep(it, through, lower):
+        for source, to, kind in LOWER_PAIRS if lower else UPPER_PAIRS:
+            if kind == through:
+                @pl.when(ja == source)
+                def _(source=source, to=to):
+                    sweep_copy(it, source, to, through, lower).start()
+
+    def await_sweep(it, lower):
+        for source, to, kind in LOWER_PAIRS if lower else UPPER_PAIRS:
+            @pl.when(ja == to)
+            def _(source=source, to=to, kind=kind):
+                sweep_copy(it, source, to, kind, lower).wait_recv()
 
     def residual_bulk(live):
         def step(j, below):
@@ -227,13 +255,7 @@
             halo_copy(it, False).start()
 
         if it == 0:
-            for i in range(len(JA_STEPS)):
-                edge_copy(i).start()
-            for lower, pairs in ((True, LOWER_MATS), (False, UPPER_MATS)):
-                for e, to in pairs:
-                    @pl.when(ja == e)
-                    def _(e=e, to=to, lower=lower):
-                        matrix_copy(e, to, lower).start()
+            send_matrices(True)
         else:
             residual_bulk(live)
 
@@ -249,6 +271,13 @@
 
         sol[0] = times(inv[0], res[0])
         sol[last] = times(inv[last], res[last])
+
+        def through_lower(it):
+            @pl.when(ja == 0)
+            def _():
+                sb[it, 1] = times(got_a, sb[it, 0])
+
+            send_sweep(it, 1, True)
 
         def lower_step(j, before):
             value = sol[j] + times(mm[j], before)
@@ -261,12 +290,17 @@
             sol[j] = value
             return value
 
-        sb[it] = lax.fori_loop(1, planes, lower_step, sol[0], unroll=True)
-        for source, to in LOWER_PAIRS:
-            @pl.when(ja == source)
-            def _(source=source, to=to):
-                sweep_copy(it, source, to, True).start()
-        lax.fori_loop(1, planes, upper_step, sol[last], unroll=True)
+        sb[it, 0] = lax.fori_loop(1, planes, lower_step, sol[0], unroll=True)
+        send_sweep(it, 0, True)
+        if it == 0:
+            send_matrices(False)
+            @pl.when(ja > 0)
+            def _():
+                for i in range(len(JA_STEPS)):
+                    edge_copy(i).start()
+        else:
+            through_lower(it)
+        sc[it] = lax.fori_loop(1, planes, upper_step, sol[last], unroll=True)
 
         for i in range(len(FACE_STEPS)):
             face_copy(it, i, True).wait_recv()
@@ -280,9 +314,84 @@
             if dz:
                 z_copy(it, dz).start()
 
+        def lower_inflow():
+            await_sweep(it, True)
+
+            @pl.when(ja == 0)
+            def _():
+                xin[...] = jnp.zeros(vec, F32)
+
+            @pl.when(ja == 1)
+            def _():
+                xin[...] = bx[it, 0]
+
+            @pl.when(ja == 2)
+            def _():
+                xin[...] = bx[it, 1] + times(got_a, bx[it, 0])
+
+            @pl.when(ja == 3)
+            def _():
+                xin[...] = bx[it, 2] + times(got_a, bx[it, 1] + bx[it, 0])
+
+            sc[it] += times(hh[0], xin[...])
+            send_sweep(it, 0, False)
+
+
+        def ghost_response():
+            for dz in Z_STEPS:
+                z_copy(it, dz).wait_recv()
+            ghosts = chosen[it, 0]
+            for dz in Z_STEPS:
+                ghosts += ghost_in[it, dz]
+            for m in range(planes * nvar):
+                gres[m // nvar, m % nvar] = ghost_weight * unpack(ghosts, m)
+
+            def ghost_start(j, carry):
+                mine = gres[j]
+                res[j] += mine
+                gres[j] = times(inv[j], mine)
+                return carry
+
+            lax.fori_loop(0, planes, ghost_start, 0, unroll=4)
+
+            def ghost_lower(j, before):
+                value = gres[j] + times(mm[j], before)
+                gres[j] = value
+                return value
+
+            def ghost_upper(s, after):
+                j = last - s
+                value = gres[j] + times(nn[j], after)
+                sol[j] += value
+                return value
+
+            bottom = lax.fori_loop(1, planes, ghost_lower, gres[0], unroll=True)
+            sol[last] += bottom
+            top = lax.fori_loop(1, planes, ghost_upper, bottom, unroll=True)
+            packet = jnp.zeros((depth_k, width), F32)
+            for v in range(nvar):
+                packet = pack(bottom[v], v, packet)
+                packet = pack(top[v], nvar + v, packet)
+            small[it, ja] = packet
+            for i in range(len(JA_STEPS)):
+                small_copy(it, i, False).start()
+
+
+        if it == 0:
+            await_matrices(0, True)
+            through_lower(it)
+            await_matrices(2, True)
+            pl.when(ja < NX - 1)(lower_inflow)
+            ghost_response()
+            await_matrices(NX - 1, True)
+            pl.when(ja == NX - 1)(lower_inflow)
+        else:
+            lower_inflow()
+            ghost_response()
+
         if it == 0:
             for i in range(len(JA_STEPS)):
-                edge_arrival(i).wait_recv()
+                pl.when(ja != JA_STEPS[i])(edge_arrival(i).wait_recv)
 
             def spread(m, carry):
                 row, col = m // nvar, m % nvar
@@ -293,94 +402,26 @@
                 return carry
 
             lax.fori_loop(0, nvar * nvar, spread, 0, unroll=5)
-            for lower, pairs in ((True, LOWER_MATS), (False, UPPER_MATS)):
-                for e, to in pairs:
-                    @pl.when(ja == to)
-                    def _(e=e, to=to, lower=lower):
-                        matrix_copy(e, to, lower).wait_recv()
-
-        for source, to in LOWER_PAIRS:
-            @pl.when(ja == to)
-            def _(source=source, to=to):
-                sweep_copy(it, source, to, True).wait_recv()
+        if it == 0:
+            await_matrices(1, False)
+            await_matrices(0, False)
+        await_sweep(it, False)
+
+        @pl.when(ja == 3)
+        def _():
+            yin[...] = jnp.zeros(vec, F32)
+
+        @pl.when(ja == 2)
+        def _():
+            yin[...] = cy[it, 3]
+
+        @pl.when(ja == 1)
+        def _():
+            yin[...] = cy[it, 2] + times(got_b[1], cy[it, 3])
 
         @pl.when(ja == 0)
         def _():
-            xin[...] = jnp.zeros(vec, F32)
-
-        @pl.when(ja > 0)
-        def _():
-            xin[...] = bx[it, 0]
-
-        for e in (1, 2):
-            @pl.when(ja > e)
-            def _(e=e):
-                xin[...] = bx[it, e] + times(got_a[e - 1], xin[...])
-
-        sc[it] = sol[0] + times(hh[0], xin[...])
-        for source, to in UPPER_PAIRS:
-            @pl.when(ja == source)
-            def _(source=source, to=to):
-                sweep_copy(it, source, to, False).start()
-
-        for dz in Z_STEPS:
-            z_copy(it, dz).wait_recv()
-        ghosts = chosen[it, 0]
-        for dz in Z_STEPS:
-            ghosts += ghost_in[it, dz]
-        for m in range(planes * nvar):
-            gres[m // nvar, m % nvar] = ghost_weight * unpack(ghosts, m)
-
-        def ghost_start(j, carry):
-            mine = gres[j]
-            res[j] += mine
-            gres[j] = times(inv[j], mine)
-            return carry
-
-        lax.fori_loop(0, planes, ghost_start, 0, unroll=4)
-        if it == ITERS - 1:
-            out_res = pltpu.make_async_copy(res, resid_hbm, out_sem.at[0])
-            out_res.start()
-
-        def ghost_lower(j, before):
-            value = gres[j] + times(mm[j], before)
-            gres[j] = value
-            return value
-
-        def ghost_upper(s, after):
-            j = last - s
-            value = gres[j] + times(nn[j], after)
-            sol[j] += value
-            return value
-
-        bottom = lax.fori_loop(1, planes, ghost_lower, gres[0], unroll=True)
-        sol[last] += bottom
-        top = lax.fori_loop(1, planes, ghost_upper, bottom, unroll=True)
-        packet = jnp.zeros((depth_k, width), F32)
-        for v in range(nvar):
-            packet = pack(bottom[v], v, packet)
-            packet = pack(top[v], nvar + v, packet)
-        small[it, ja] = packet
-        for i in range(len(JA_STEPS)):
-            small_copy(it, i, False).start()
-
-        for source, to in UPPER_PAIRS:
-            @pl.when(ja == to)
-            def _(source=source, to=to):
-                sweep_copy(it, source, to, False).wait_recv()
-
-        @pl.when(ja == NX - 1)
-        def _():
-            yin[...] = jnp.zeros(vec, F32)
-
-        @pl.when(ja < NX - 1)
-        def _():
-            yin[...] = cy[it, NX - 1]
-
-        for e in (2, 1):
-            @pl.when(ja < e)
-            def _(e=e):
-                yin[...] = cy[it, e] + times(got_b[e - 1], yin[...])
+            yin[...] = cy[it, 1] + times(got_b[0], cy[it, 2] + times(got_b[1], cy[it, 3]))
 
         @pl.when(ja > 0)
         def _():
@@ -422,8 +463,6 @@
         if it < ITERS - 1:
             pack_faces(it + 1)
 
-    out_state = pltpu.make_async_copy(cur, state_hbm, out_sem.at[1])
-    out_state.start()
     for it in range(ITERS):
         for i in range(len(FACE_STEPS)):
             face_copy(it, i, False).wait_send()
@@ -432,19 +471,32 @@
         for i in range(len(JA_STEPS)):
             small_copy(it, i, False).wait_send()
         for lower, pairs in ((True, LOWER_PAIRS), (False, UPPER_PAIRS)):
-            for source, to in pairs:
+            for source, to, kind in pairs:
                 @pl.when(ja == source)
-                def _(source=source, to=to, lower=lower):
-                    sweep_copy(it, source, to, lower).wait_send()
-    for i in range(len(JA_STEPS)):
-        edge_copy(i).wait_send()
+                def _(source=source, to=to, kind=kind, lower=lower):
+                    sweep_copy(it, source, to, kind, lower).wait_send()
+
+    @pl.when(ja > 0)
+    def _():
+        for i in range(len(JA_STEPS)):
+            edge_copy(i).wait_send()
+
     for lower, pairs in ((True, LOWER_MATS), (False, UPPER_MATS)):
         for e, to in pairs:
             @pl.when(ja == e)
             def _(e=e, to=to, lower=lower):
                 matrix_copy(e, to, lower).wait_send()
-    out_res.wait()
-    out_state.wait()
+
+
+def write_out(state_ref, resid_ref, state_out, resid_out, sems):
+    copies = [
+        pltpu.make_async_copy(state_ref, state_out, sems.at[0]),
+        pltpu.make_async_copy(resid_ref, resid_out, sems.at[1]),
+    ]
+    for copy in copies:
+        copy.start()
+    for copy in copies:
+        copy.wait()
 
 
 def per_device(flow_state, forcing, diag_block, lower_jac, upper_jac, block_inv, east_zone, zone_depth):
@@ -460,23 +512,31 @@
     ints = pltpu.SMEM(east_zone.shape, jnp.int32)
     state, resid = pl.pallas_call(
         kernel,
-        out_shape=[jax.ShapeDtypeStruct((planes,) + vec, F32)] * 2,
+        out_shape=[pltpu.VMEM((planes,) + vec, F32)] * 2,
         in_specs=[pl.BlockSpec(memory_space=pltpu.HBM)] * 8,
-        out_specs=[pl.BlockSpec(memory_space=pltpu.HBM)] * 2,
+        out_specs=[pl.BlockSpec(memory_space=pltpu.VMEM)] * 2,
         scratch_shapes=[ints, ints]
-        + [vmem(planes, *vec)] * 2 + [vmem(planes, *mat)] * 4
-        + [vmem(planes, *mat)] * 5 + [vmem(planes, *vec)] * 3 + [vmem(2, *mat)] * 2
+        + [vmem(planes, *vec)] + [vmem(planes, *mat)] * 4
+        + [vmem(planes, *mat)] * 5 + [vmem(planes, *vec)] * 2 + [vmem(*mat), vmem(2, *mat)]
         + [vmem(NX, 3, *tile), vmem(NX, 3, *mat), vmem(2, NY, *tile), vmem(2, NY, *tile)]
         + [vmem(ITERS, NZ, *tile)] * 2 + [vmem(ITERS, 2, *vec)]
-        + [vmem(ITERS, *vec)] * 2 + [vmem(ITERS, NX, *vec)] * 2 + [vmem(*vec)] * 2
+        + [vmem(ITERS, 2, *vec), vmem(ITERS, *vec)] + [vmem(ITERS, NX, *vec)] * 2 + [vmem(*vec)] * 2
         + [vmem(ITERS, NX, *tile), vmem(NX, 2 * nvar, *tile)]
         + [dma((8,)), dma((ITERS, 7)), dma((ITERS, 7)), dma((ITERS, NZ)), dma((ITERS, NZ)), dma((ITERS, 2)), dma((ITERS, 2))]
-        + [dma((NX,)), dma((2,)), dma((NX,)), dma((2,)), dma((3,)), dma((3,))]
-        + [dma((ITERS, NX))] * 4 + [dma((ITERS, 3))] * 2 + [dma((2,))],
+        + [dma((2,)), dma, dma((2,)), dma((2,)), dma((3,)), dma((3,))]
+        + [dma((ITERS, NX))] * 4 + [dma((ITERS, 3))] * 2,
         compiler_params=pltpu.CompilerParams(
-            collective_id=0, has_side_effects=True, vmem_limit_bytes=64 * 2**20 - 2**17),
+            collective_id=0, has_side_effects=True, vmem_limit_bytes=63 * 2**20),
         name="ssor",
     )(east_zone, zone_depth, flow_state[0], forcing[0], diag_block[0], lower_jac[0], upper_jac[0], block_inv[0])
+    state, resid = pl.pallas_call(
+        write_out,
+        out_shape=[jax.ShapeDtypeStruct((planes,) + vec, F32)] * 2,
+        in_specs=[pl.BlockSpec(memory_space=pltpu.VMEM)] * 2,
+        out_specs=[pl.BlockSpec(memory_space=pltpu.HBM)] * 2,
+        scratch_shapes=[dma((2,))],
+        name="write_out",
+    )(*(pltpu.with_memory_space_constraint(array, pltpu.VMEM) for array in (state, resid)))
     return state[None], resid[None]
 
 

time: 50.6 us -> 44.4 us (0.88); the launches traced: 50.4 us -> 43.6 us
  local copies, waits for them, and re-layouts: 3.44 us -> 0 us
  Pallas kernels: 46.3 us -> 42.9 us
    unnamed x2 -> x0, local copies, waits for them, and re-layouts: 3.44 us -> none
    pallas_call x1 -> x2, Pallas kernels: 46.3 us -> 42.9 us  [the longest x1 42.1 us: per_device(): pl.pallas_call(kernel, out_shape=[pltpu.VMEM((planes,) + vec, F32)] * 2,...]
where the time goes in v2:
time: 44.4 us; the launch traced here: 43.6 us
  Pallas kernels  42.9 us (97%)
  between operations  0.64 us (1%)
    pallas_call x1, Pallas kernels, per_device(): pl.pallas_call(kernel, out_shape=[pltpu.VMEM((planes,) + vec, F32)] * 2,...  42.1 us

profile of v2, /device:TPU:1, one launch (start us, length us, event | category | flops | bytes accessed | tf_op | source)
XLA Modules:
  0.0 43.6 jit_solution(16686517625556570833)
XLA Ops:
  0.6 42.1 %ssor.1 = (f32[8,5,16,128]{3,2,1,0:T(8,128)S(1)}, f32[8,5,16,128]{3,2,1,0:T(8,128)S(1)}) custom-call(s32[64]{0:T(128)} %east_hbm.1, s32[64]{0:T(128)} %depth_hbm.1, f32[8,5,16,128]{3,2,1,0:T(8,128)} %bitcast.12, f32[8,5,16,128]{3,2,1,0:T(8,128)} %bitcast.13, f32[8,5,5,16,128]{4,3,2,1,0:T(8,128)} %bitcast.8, f32[8,5,5,16,128]{4,3,2,1,0:T(8,128)} %bitcast.9, ...), custom_call_target="tpu_custom_call" | custom-call | tf_op jit(solution)/shard_map/ssor/pallas_call | solution.py:513
  42.7 0.9 %write_out.1 = (f32[8,5,16,128]{3,2,1,0:T(8,128)}, f32[8,5,16,128]{3,2,1,0:T(8,128)}) custom-call(f32[8,5,16,128]{3,2,1,0:T(8,128)S(1)} %get-tuple-element.6.state_ref, f32[8,5,16,128]{3,2,1,0:T(8,128)S(1)} %get-tuple-element.7.resid_ref), custom_call_target="tpu_custom_call" | custom-call | tf_op jit(solution)/shard_map/write_out/pallas_call | solution.py:532

commit v3 on v2

--- a/solution.py
+++ b/solution.py
@@ -26,7 +26,7 @@
     east_ref, depth_ref, forc, diag, low, upp, inv,
     mm, nn, pp, rr, hh, gres, sol, got_a, got_b,
     edge_pack, edge_mat, face0, face1, chosen, ghost_in, halo,
-    sb, sc, bx, cy, xin, yin, small, small_vec,
+    sb, sc, bx, cy, xin, yin, ghost_x, ghost_y, small, small_vec,
     load_sem, face_s, face_r, z_s, z_r, halo_s, halo_r,
     a_s, a_r, b_s, b_r, e_s, e_r, x_s, x_r, u_s, u_r, g_s, g_r,
 ):
@@ -230,12 +230,14 @@
         return carry
 
     lax.fori_loop(1, planes, through, 0)
-    packets = [jnp.zeros((depth_k, width), F32)] * 3
+    packets = [jnp.zeros((depth_k, width), F32)] * 2
     for row in range(nvar):
         for col in range(nvar):
-            for i, product in enumerate((pp.at[last], rr.at[0], hh.at[0])):
-                packets[i] = pack(product[row, col], row * nvar + col, packets[i])
-    for i in range(3):
+            m = row * nvar + col
+            packets[0] = pack(pp[last, row, col], m, packets[0])
+            packets[0] = pack(rr[0, row, col], nvar * nvar + m, packets[0])
+            packets[1] = pack(hh[0, row, col], m, packets[1])
+    for i in range(2):
         edge_pack[ja, i] = packets[i]
     loads[6].wait()
     loads[7].wait()
@@ -396,47 +398,13 @@
             def spread(m, carry):
                 row, col = m // nvar, m % nvar
                 for e in (1, 2, 3):
-                    for i in range(3):
-                        if e < 3 or i == 2:
-                            edge_mat[e, i, row, col] = unpack(edge_pack[e, i], m)
+                    edge_mat[e, 2, row, col] = unpack(edge_pack[e, 1], m)
+                    if e < 3:
+                        edge_mat[e, 0, row, col] = unpack(edge_pack[e, 0], m)
+                        edge_mat[e, 1, row, col] = unpack(edge_pack[e, 0], nvar * nvar + m)
                 return carry
 
             lax.fori_loop(0, nvar * nvar, spread, 0, unroll=5)
-        if it == 0:
-            await_matrices(1, False)
-            await_matrices(0, False)
-        await_sweep(it, False)
-
-        @pl.when(ja == 3)
-        def _():
-            yin[...] = jnp.zeros(vec, F32)
-
-        @pl.when(ja == 2)
-        def _():
-            yin[...] = cy[it, 3]
-
-        @pl.when(ja == 1)
-        def _():
-            yin[...] = cy[it, 2] + times(got_b[1], cy[it, 3])
-
-        @pl.when(ja == 0)
-        def _():
-            yin[...] = cy[it, 1] + times(got_b[0], cy[it, 2] + times(got_b[1], cy[it, 3]))
-
-        @pl.when(ja > 0)
-        def _():
-            halo_copy(it, True).wait_send()
-
-        @pl.when(ja < NX - 1)
-        def _():
-            halo_copy(it, False).wait_send()
-
-        def raise_plane(j, carry):
-            cur[j] += sol[j] + times(hh[j], xin[...]) + times(rr[j], yin[...])
-            return carry
-
-        lax.fori_loop(0, planes, raise_plane, 0, unroll=2)
-
         for i in range(len(JA_STEPS)):
             small_copy(it, i, True).wait_recv()
         for e in range(NX):
@@ -452,14 +420,46 @@
         y2 = small_vec[3, high_end] + times(edge_mat[3, 2], x3)
         y1 = small_vec[2, high_end] + times(edge_mat[2, 2], x2) + times(edge_mat[2, 1], y2)
         y0 = small_vec[1, high_end] + times(edge_mat[1, 2], x1) + times(edge_mat[1, 1], y1)
-        xin[...] = jnp.where(ja == 0, 0.0, jnp.where(ja == 1, x1, jnp.where(ja == 2, x2, x3)))
-        yin[...] = jnp.where(ja == 3, 0.0, jnp.where(ja == 2, y2, jnp.where(ja == 1, y1, y0)))
-
-        def raise_edges(j, carry):
-            cur[j] += times(hh[j], xin[...]) + times(rr[j], yin[...])
+        ghost_x[...] = jnp.where(ja == 0, 0.0, jnp.where(ja == 1, x1, jnp.where(ja == 2, x2, x3)))
+        ghost_y[...] = jnp.where(ja == 3, 0.0, jnp.where(ja == 2, y2, jnp.where(ja == 1, y1, y0)))
+
+        if it == 0:
+            await_matrices(1, False)
+            await_matrices(0, False)
+        await_sweep(it, False)
+
+        @pl.when(ja == 3)
+        def _():
+            yin[...] = jnp.zeros(vec, F32)
+
+        @pl.when(ja == 2)
+        def _():
+            yin[...] = cy[it, 3]
+
+        @pl.when(ja == 1)
+        def _():
+            yin[...] = cy[it, 2] + times(got_b[1], cy[it, 3])
+
+        @pl.when(ja == 0)
+        def _():
+            yin[...] = cy[it, 1] + times(got_b[0], cy[it, 2] + times(got_b[1], cy[it, 3]))
+
+        @pl.when(ja > 0)
+        def _():
+            halo_copy(it, True).wait_send()
+
+        @pl.when(ja < NX - 1)
+        def _():
+            halo_copy(it, False).wait_send()
+
+        xin[...] += ghost_x[...]
+        yin[...] += ghost_y[...]
+
+        def raise_plane(j, carry):
+            cur[j] += sol[j] + times(hh[j], xin[...]) + times(rr[j], yin[...])
             return carry
 
-        lax.fori_loop(0, planes, raise_edges, 0, unroll=4)
+        lax.fori_loop(0, planes, raise_plane, 0, unroll=2)
         if it < ITERS - 1:
             pack_faces(it + 1)
 
@@ -518,9 +518,9 @@
         scratch_shapes=[ints, ints]
         + [vmem(planes, *vec)] + [vmem(planes, *mat)] * 4
         + [vmem(planes, *mat)] * 5 + [vmem(planes, *vec)] * 2 + [vmem(*mat), vmem(2, *mat)]
-        + [vmem(NX, 3, *tile), vmem(NX, 3, *mat), vmem(2, NY, *tile), vmem(2, NY, *tile)]
+        + [vmem(NX, 2, *tile), vmem(NX, 3, *mat), vmem(2, NY, *tile), vmem(2, NY, *tile)]
         + [vmem(ITERS, NZ, *tile)] * 2 + [vmem(ITERS, 2, *vec)]
-        + [vmem(ITERS, 2, *vec), vmem(ITERS, *vec)] + [vmem(ITERS, NX, *vec)] * 2 + [vmem(*vec)] * 2
+        + [vmem(ITERS, 2, *vec), vmem(ITERS, *vec)] + [vmem(ITERS, NX, *vec)] * 2 + [vmem(*vec)] * 4
         + [vmem(ITERS, NX, *tile), vmem(NX, 2 * nvar, *tile)]
         + [dma((8,)), dma((ITERS, 7)), dma((ITERS, 7)), dma((ITERS, NZ)), dma((ITERS, NZ)), dma((ITERS, 2)), dma((ITERS, 2))]
         + [dma((2,)), dma, dma((2,)), dma((2,)), dma((3,)), dma((3,))]

time: 44.4 us -> 43.9 us (0.989)
  no operation moved by 1% of the time
where the time goes in v3:
time: 43.9 us; the launch traced here: 43.2 us
  Pallas kernels  42.6 us (97%)
  between operations  0.64 us (1%)
    pallas_call x1, Pallas kernels, per_device(): pl.pallas_call(kernel, out_shape=[pltpu.VMEM((planes,) + vec, F32)] * 2,...  41.7 us

profile of v3, /device:TPU:1, one launch (start us, length us, event | category | flops | bytes accessed | tf_op | source)
XLA Modules:
  0.0 43.2 jit_solution(7203346606114281054)
XLA Ops:
  0.6 41.7 %ssor.1 = (f32[8,5,16,128]{3,2,1,0:T(8,128)S(1)}, f32[8,5,16,128]{3,2,1,0:T(8,128)S(1)}) custom-call(s32[64]{0:T(128)} %east_hbm.1, s32[64]{0:T(128)} %depth_hbm.1, f32[8,5,16,128]{3,2,1,0:T(8,128)} %bitcast.12, f32[8,5,16,128]{3,2,1,0:T(8,128)} %bitcast.13, f32[8,5,5,16,128]{4,3,2,1,0:T(8,128)} %bitcast.8, f32[8,5,5,16,128]{4,3,2,1,0:T(8,128)} %bitcast.9, ...), custom_call_target="tpu_custom_call" | custom-call | tf_op jit(solution)/shard_map/ssor/pallas_call | solution.py:513
  42.4 0.9 %write_out.1 = (f32[8,5,16,128]{3,2,1,0:T(8,128)}, f32[8,5,16,128]{3,2,1,0:T(8,128)}) custom-call(f32[8,5,16,128]{3,2,1,0:T(8,128)S(1)} %get-tuple-element.6.state_ref, f32[8,5,16,128]{3,2,1,0:T(8,128)S(1)} %get-tuple-element.7.resid_ref), custom_call_target="tpu_custom_call" | custom-call | tf_op jit(solution)/shard_map/write_out/pallas_call | solution.py:532

commit v4 on v3

--- a/solution.py
+++ b/solution.py
@@ -345,21 +345,16 @@
             ghosts = chosen[it, 0]
             for dz in Z_STEPS:
                 ghosts += ghost_in[it, dz]
-            for m in range(planes * nvar):
-                gres[m // nvar, m % nvar] = ghost_weight * unpack(ghosts, m)
-
-            def ghost_start(j, carry):
-                mine = gres[j]
-                res[j] += mine
-                gres[j] = times(inv[j], mine)
-                return carry
-
-            lax.fori_loop(0, planes, ghost_start, 0, unroll=4)
-
-            def ghost_lower(j, before):
-                value = gres[j] + times(mm[j], before)
+            bottom = None
+            for j in range(planes):
+                mine = [ghost_weight * unpack(ghosts, j * nvar + v) for v in range(nvar)]
+                value = times(inv[j], mine)
+                if j:
+                    value += times(mm[j], bottom)
                 gres[j] = value
-                return value
+                bottom = value
+                for v in range(nvar):
+                    res[j, v] += mine[v]
 
             def ghost_upper(s, after):
                 j = last - s
@@ -367,7 +362,6 @@
                 sol[j] += value
                 return value
 
-            bottom = lax.fori_loop(1, planes, ghost_lower, gres[0], unroll=True)
             sol[last] += bottom
             top = lax.fori_loop(1, planes, ghost_upper, bottom, unroll=True)
             packet = jnp.zeros((depth_k, width), F32)
@@ -388,8 +382,9 @@
             await_matrices(NX - 1, True)
             pl.when(ja == NX - 1)(lower_inflow)
         else:
-            lower_inflow()
+            pl.when(ja < NX - 1)(lower_inflow)
             ghost_response()
+            pl.when(ja == NX - 1)(lower_inflow)
 
         if it == 0:
             for i in range(len(JA_STEPS)):
@@ -452,16 +447,17 @@
         def _():
             halo_copy(it, False).wait_send()
 
-        xin[...] += ghost_x[...]
-        yin[...] += ghost_y[...]
-
-        def raise_plane(j, carry):
-            cur[j] += sol[j] + times(hh[j], xin[...]) + times(rr[j], yin[...])
-            return carry
-
-        lax.fori_loop(0, planes, raise_plane, 0, unroll=2)
+        inflow = xin[...] + ghost_x[...]
+        backflow = yin[...] + ghost_y[...]
+        packet = jnp.zeros((depth_k, width), F32)
+        for j in range(planes):
+            value = cur[j] + sol[j] + times(hh[j], inflow) + times(rr[j], backflow)
+            cur[j] = value
+            if it < ITERS - 1:
+                for v in range(nvar):
+                    packet = pack(value[v], j * nvar + v, packet)
         if it < ITERS - 1:
-            pack_faces(it + 1)
+            faces[it + 1][c, y] = packet
 
     for it in range(ITERS):
         for i in range(len(FACE_STEPS)):

time: 43.9 us -> 43.7 us (level)
  no operation moved by 1% of the time
where the time goes in v4:
time: 43.7 us; the launch traced here: 43.3 us
  Pallas kernels  42.7 us (98%)
  between operations  0.64 us (1%)
    pallas_call x1, Pallas kernels, per_device(): pl.pallas_call(kernel, out_shape=[pltpu.VMEM((planes,) + vec, F32)] * 2,...  41.8 us

profile of v4, /device:TPU:1, one launch (start us, length us, event | category | flops | bytes accessed | tf_op | source)
XLA Modules:
  0.0 43.3 jit_solution(17024244216870961971)
XLA Ops:
  0.6 41.8 %ssor.1 = (f32[8,5,16,128]{3,2,1,0:T(8,128)S(1)}, f32[8,5,16,128]{3,2,1,0:T(8,128)S(1)}) custom-call(s32[64]{0:T(128)} %east_hbm.1, s32[64]{0:T(128)} %depth_hbm.1, f32[8,5,16,128]{3,2,1,0:T(8,128)} %bitcast.12, f32[8,5,16,128]{3,2,1,0:T(8,128)} %bitcast.13, f32[8,5,5,16,128]{4,3,2,1,0:T(8,128)} %bitcast.8, f32[8,5,5,16,128]{4,3,2,1,0:T(8,128)} %bitcast.9, ...), custom_call_target="tpu_custom_call" | custom-call | tf_op jit(solution)/shard_map/ssor/pallas_call | solution.py:509
  42.5 0.9 %write_out.1 = (f32[8,5,16,128]{3,2,1,0:T(8,128)}, f32[8,5,16,128]{3,2,1,0:T(8,128)}) custom-call(f32[8,5,16,128]{3,2,1,0:T(8,128)S(1)} %get-tuple-element.6.state_ref, f32[8,5,16,128]{3,2,1,0:T(8,128)S(1)} %get-tuple-element.7.resid_ref), custom_call_target="tpu_custom_call" | custom-call | tf_op jit(solution)/shard_map/write_out/pallas_call | solution.py:528
